TPU v7x, 256 devices: a whole 4x4x8 slice. The times are simulated.
256 devices in a mesh: chan: 8 (over x, y_hi), seg: 32 (over y_lo, z, core).
Axes of the slice: x: 4, y: 4 (y_hi: 2, y_lo: 2; y = y_hi * 2 + y_lo), z: 8, core: 2. Of those that a mesh axis runs over, the one named last changes fastest.
Arguments:
- spectra: bfloat16 [128, 2, 200, 1024], P('seg', None, None, 'chan'), may hold values from -6 to 6
- match: int32 [3, 8], replicated, may hold values from 0 to 7, as said below
- counts: int32 [32], P('seg'), may hold values from 1 to 4, as said below
Outputs:
- correlations: float32 [3, 51, 1024, 128], P(None, None, ('chan', 'seg'))
Inputs may be any that keep to these rules, and one draw needn't show every extreme that they name: In each round partnership is mutual (match[r, match[r, c]] = c); a block may be its own partner; rounds are drawn independently and may repeat. `counts`: some group has all 4 slots valid.
All inputs are finite; a program needn't handle non-finite values.
Results may differ from a plain program's by a relative error of at most 0.0003.
Values may be sent and summed in bfloat16 or wider, within the bound.
No kernel may reach another device: no remote copies, remote signals or barrier semaphores. Data moves between devices by JAX's collectives and lax.ppermute only.
A program may use at most 128 MiB of HBM per device.

v0:
```python
import jax
import jax.numpy as jnp
from jax import lax
from jax.sharding import PartitionSpec as P

LAGS = 51
SAMPLES = 3000
ROUNDS = 3


def lag_table(lags, freq):
    lag = jnp.arange(lags, dtype=jnp.float32)[:, None] - jnp.float32(lags // 2)
    bins = jnp.arange(freq, dtype=jnp.float32)[None, :] + 1.0
    angle = 2.0 * jnp.pi * bins * lag / jnp.float32(SAMPLES)
    return jnp.concatenate([jnp.cos(angle), -jnp.sin(angle)], axis=1)


def on_device(spectra, match, counts):
    seg_slots = spectra.shape[0]
    freq = spectra.shape[2]
    block = spectra.shape[3]
    whole = lax.all_gather(spectra, "chan", axis=3, tiled=True)
    total = lax.psum(jnp.sum(counts).astype(jnp.float32), "seg")
    valid = (jnp.arange(seg_slots, dtype=jnp.int32) < counts[0]).astype(jnp.bfloat16)
    own = spectra * valid[:, None, None, None]
    table = lag_table(LAGS, freq)
    here = lax.axis_index("chan")
    scale = 1.0 / jnp.sqrt(total * jnp.float32(freq))
    pieces = []
    for r in range(ROUNDS):
        partner = match[r, here]
        other = lax.dynamic_slice_in_dim(whole, partner * block, block, 3)
        rotated = jnp.stack([-other[:, 1], other[:, 0]], axis=1)
        real = jnp.einsum("spfa,spfb->fab", own, other, preferred_element_type=jnp.float32)
        imag = jnp.einsum("spfa,spfb->fab", own, rotated, preferred_element_type=jnp.float32)
        both = jnp.concatenate([real, imag], axis=0).reshape(2 * freq, block * block)
        lagged = jnp.dot(table, both, precision=lax.Precision.HIGHEST).reshape(LAGS, block, block)
        pieces.append(lax.psum_scatter(lagged, "seg", scatter_dimension=1, tiled=True))
    stacked = jnp.stack(pieces, axis=0)
    return stacked * scale


def solution(mesh):
    return jax.shard_map(
        on_device,
        mesh=mesh,
        in_specs=(P("seg", None, None, "chan"), P(), P("seg")),
        out_specs=P(None, None, ("chan", "seg"), None),
        check_vma=False,
    )
```

profile of v0, /device:TPU:1, one launch (start us, length us, event | category | flops | bytes accessed | tf_op | source)
XLA Modules:
  0.0 526.5 jit_solution(4802990797344745401)
XLA Ops:
  6.5 0.0 all-gather.2.cloned.1.call-start
  6.5 1.9 copy.12
  8.4 0.0 all-gather.2.cloned.1.call-update
  8.5 0.0 reduce-scatter.6.cloned.1.call-start
  8.5 1.5 constant_dynamic-slice_fusion.3
  12.7 0.3 fusion.21
  12.9 1.1 broadcast_multiply_fusion
  14.1 86.9 %all-gather.2.cloned.1.call-done = bf16[4,2,200,1024]{3,0,1,2:T(4,128)(2,1)} async-done(((bf16[4,2,200,128]{3,0,1,2:T(4,128)(2,1)}), bf16[4,2,200,1024]{3,0,1,2:T(4,128)(2,1)}) %all-gather.2.cloned.1.call-update) | async-done | bytes 3276816 | tf_op jit(solution)/shard_map/all_gather | solution.py:22
  101.0 1.9 dynamic-slice_negate_fusion.2
  102.9 2.2 convolution_bitcast_fusion.2
  105.1 3.2 convolution_bitcast_fusion.3
  108.3 12.4 %pad_maximum_fusion.1 = f32[400,128,128]{2,1,0:T(8,128)} fusion(f32[200,128,128]{2,1,0:T(8,128)S(1)} %convolution_bitcast_fusion.2, f32[200,128,128]{2,1,0:T(8,128)S(1)} %convolution_bitcast_fusion.3), kind=kLoop, calls=%fused_computation.13 | loop fusion | flops 6553600 | bytes 52428800 | tf_op jit(solution)/shard_map/concatenate | solution.py:36
  120.8 41.6 %fusion.3 = f32[51,128,128]{2,0,1:T(8,128)} fusion(f32[51,200]{1,0:T(8,128)S(1)} %get-tuple-element.15, f32[51,200]{1,0:T(8,128)S(1)} %get-tuple-element.14, f32[50,8,128,128]{3,2,1,0:T(8,128)} %bitcast.72), kind=kOutput, calls=%fused_computation.6 | convolution fusion | flops 4010823680 | bytes 29638336 | tf_op jit(solution)/shard_map/dot_general | solution.py:37
  162.4 0.0 reduce-scatter.6.cloned.1.call-update
  162.4 0.0 reduce-scatter.4.cloned.1.call-start
  162.4 2.2 convolution_bitcast_fusion.4
  164.7 3.2 convolution_bitcast_fusion.5
  167.9 12.4 %pad_maximum_fusion = f32[400,128,128]{2,1,0:T(8,128)} fusion(f32[200,128,128]{2,1,0:T(8,128)S(1)} %convolution_bitcast_fusion.4, f32[200,128,128]{2,1,0:T(8,128)S(1)} %convolution_bitcast_fusion.5), kind=kLoop, calls=%fused_computation.12 | loop fusion | flops 6553600 | bytes 52428800 | tf_op jit(solution)/shard_map/concatenate | solution.py:36
  180.3 41.6 %fusion.6 = f32[51,128,128]{2,0,1:T(8,128)} fusion(f32[51,200]{1,0:T(8,128)S(1)} %get-tuple-element.15, f32[51,200]{1,0:T(8,128)S(1)} %get-tuple-element.14, f32[50,8,128,128]{3,2,1,0:T(8,128)} %bitcast.73), kind=kOutput, calls=%fused_computation.9 | convolution fusion | flops 4010823680 | bytes 29638336 | tf_op jit(solution)/shard_map/dot_general | solution.py:37
  222.0 0.0 reduce-scatter.4.cloned.1.call-update
  222.0 0.0 reduce-scatter.8.cloned.1.call-start
  222.0 2.2 convolution_bitcast_fusion
  224.3 3.2 convolution_bitcast_fusion.1
  227.5 12.4 %pad_maximum_fusion.2 = f32[400,128,128]{2,1,0:T(8,128)} fusion(f32[200,128,128]{2,1,0:T(8,128)S(1)} %convolution_bitcast_fusion, f32[200,128,128]{2,1,0:T(8,128)S(1)} %convolution_bitcast_fusion.1), kind=kLoop, calls=%fused_computation.14 | loop fusion | flops 6553600 | bytes 52428800 | tf_op jit(solution)/shard_map/concatenate | solution.py:36
  239.9 41.2 %fusion = f32[51,128,128]{2,0,1:T(8,128)} fusion(f32[51,200]{1,0:T(8,128)S(1)} %get-tuple-element.15, f32[51,200]{1,0:T(8,128)S(1)} %get-tuple-element.14, f32[50,8,128,128]{3,2,1,0:T(8,128)} %bitcast.71), kind=kOutput, calls=%fused_computation.3 | convolution fusion | flops 4010823680 | bytes 29638336 | tf_op jit(solution)/shard_map/dot_general | solution.py:37
  281.2 0.0 reduce-scatter.8.cloned.1.call-update
  281.2 53.9 %psum.7 = f32[]{:T(128)} all-reduce(f32[]{:T(128)S(6)} %convert_element_type.11), channel_id=1, replica_groups=mesh['chan'=8,'seg'=32] {'seg'}, use_global_device_ids=true, to_apply=%region_3.0 | all-reduce | flops 1 | bytes 8 | tf_op jit(solution)/shard_map/psum | solution.py:23
  335.8 0.0 reduce-scatter.6.cloned.1.call-done
  335.8 63.0 %reduce-scatter.4.cloned.1.call-done = f32[51,4,128]{2,0,1:T(8,128)} async-done(((f32[51,128,128]{2,0,1:T(8,128)}), f32[51,4,128]{2,0,1:T(8,128)}) %reduce-scatter.4.cloned.1.call-update) | async-done | bytes 104464 | tf_op jit(solution)/shard_map/reduce_scatter | solution.py:38
  398.8 119.1 %reduce-scatter.8.cloned.1.call-done = f32[51,4,128]{2,0,1:T(8,128)} async-done(((f32[51,128,128]{2,0,1:T(8,128)}), f32[51,4,128]{2,0,1:T(8,128)}) %reduce-scatter.8.cloned.1.call-update) | async-done | bytes 104464 | tf_op jit(solution)/shard_map/reduce_scatter | solution.py:38
  517.9 1.0 maximum_multiply_fusion
  518.9 0.8 copy.22
  (3 shorter events, 0.0 us)
Async XLA Ops:
  6.5 94.4 %all-gather.2.cloned.1.call-start = ((), (), s32[]{:S(2)}) async-start(), calls=%async_computation.3 | async-start | bytes 3686400 | tf_op jit(solution)/shard_map/all_gather | solution.py:22
  8.5 327.3 %reduce-scatter.6.cloned.1.call-start = ((), (), s32[]{:S(2)}) async-start(), calls=%async_computation.5 | async-start | bytes 3784704 | tf_op jit(solution)/shard_map/reduce_scatter | solution.py:38
  162.4 236.4 %reduce-scatter.4.cloned.1.call-start = ((), (), s32[]{:S(2)}) async-start(), calls=%async_computation.4 | async-start | bytes 3784704 | tf_op jit(solution)/shard_map/reduce_scatter | solution.py:38
  222.0 295.9 %reduce-scatter.8.cloned.1.call-start = ((), (), s32[]{:S(2)}) async-start(), calls=%async_computation.6 | async-start | bytes 3784704 | tf_op jit(solution)/shard_map/reduce_scatter | solution.py:38
Sparse Core Ops, SparseCore 0:
  9.8 91.1 all-gather.1
  162.5 116.3 reduce-scatter.5
  281.6 117.1 reduce-scatter.3
  401.2 116.6 reduce-scatter.7
where the time goes:
time: 535 us; the launch traced here: 526 us
  waiting for transfers between devices  269 us (50%)
  matrix products  141 us (26%)
  blocking collectives  53.9 us (10%)
  other arithmetic  41.6 us (8%)
  between operations  16.7 us (3%)
    reduce_scatter x3, waiting for transfers between devices, on_device(): lax.psum_scatter(lagged, 'seg', scatter_dimension=1, tiled=True)  182 us
    dot_general x3, matrix products, on_device(): jnp.dot(table, both, precision=lax.Precision.HIGHEST)  124 us
    all_gather x1, waiting for transfers between devices, on_device(): whole = lax.all_gather(spectra, 'chan', axis=3, tiled=True)  86.9 us
    psum x1, blocking collectives, on_device(): total = lax.psum(jnp.sum(counts).astype(jnp.float32), 'seg')  53.9 us
    concatenate x3, other arithmetic, on_device(): jnp.concatenate([real, imag], axis=0).reshape(2 * freq, block * block)  37.3 us
  transfers between devices with their start and end apart: 4, of which 3 were waited for; matrix products, arithmetic and copies ran while one was open for 23% of the time, Pallas kernels for 0%

commit v1 on v0

v1 whole, which is shorter than its diff:
```python
import jax
import jax.numpy as jnp
import numpy as np
from jax import lax
from jax.experimental import pallas as pl
from jax.experimental.pallas import tpu as pltpu
from jax.sharding import PartitionSpec as P

LAGS = 51
SAMPLES = 3000
ROUNDS = 3
HALF = LAGS // 2
ROWS = 32


def tables(freq, bins):
    lag = np.arange(ROWS, dtype=np.float64)[:, None]
    f = np.arange(bins, dtype=np.float64)[None, :] + 1.0
    angle = 2.0 * np.pi * f * lag / SAMPLES
    live = (np.arange(bins)[None, :] < freq) & (np.arange(ROWS)[:, None] <= HALF)
    return (
        np.where(live, np.cos(angle), 0.0).astype(np.float32),
        np.where(live, np.sin(angle), 0.0).astype(np.float32),
    )


def cross_kernel(match, x, out, turned):
    blocks, depth, block = x.shape
    tile = 2 * (block // 32)
    sources = depth // tile

    row = lax.broadcasted_iota(jnp.int32, (2 * block, 2 * block), 0)
    col = lax.broadcasted_iota(jnp.int32, (2 * block, 2 * block), 1)
    half = tile // 2
    channel = (row // tile) * half + row % half
    part = (row % tile) // half
    order = (col == part * block + channel).astype(jnp.bfloat16)

    def turn(c, _):
        own = x[c]
        groups = own.astype(jnp.float32).reshape(sources, tile, block)
        swapped = jnp.concatenate([groups[:, half:], -groups[:, :half]], axis=1)
        both = jnp.concatenate([own, swapped.reshape(depth, block).astype(jnp.bfloat16)], axis=1)
        turned[c] = lax.dot_general(
            order, both, (((1,), (1,)), ((), ())), preferred_element_type=jnp.float32
        ).astype(jnp.bfloat16)
        return 0

    lax.fori_loop(0, blocks, turn, 0)

    def one(c, _):
        for r in range(ROUNDS):
            product = jnp.dot(turned[c], x[match[r, c]], preferred_element_type=jnp.float32)
            out[pl.ds(c * 32, 32), r * tile : (r + 1) * tile, :] = product.reshape(32, tile, block)
        return 0

    lax.fori_loop(0, blocks, one, 0)


def split(v):
    high = v.astype(jnp.bfloat16)
    return high, (v - high.astype(jnp.float32)).astype(jnp.bfloat16)


def lag_kernel(freq, cos, sin, x, out):
    bins = cos.shape[1]
    rows = x.shape[0] // bins
    tile = rows // ROUNDS
    half = tile // 2
    cos_high, cos_low = split(cos[...])
    sin_high, sin_low = split(sin[...])
    cos_both = jnp.concatenate([cos_high, cos_low], axis=0)
    sin_both = jnp.concatenate([sin_high, sin_low], axis=0)

    def apply(both, top, v):
        high, low = split(v)
        first = jnp.dot(both, high, preferred_element_type=jnp.float32)
        return first[:ROWS] + first[ROWS:] + jnp.dot(top, low, preferred_element_type=jnp.float32)

    for r in range(ROUNDS):
        for a in range(half):
            at = r * tile + a
            real = x[pl.ds(at, bins, stride=rows), :]
            imag = x[pl.ds(at + half, bins, stride=rows), :]
            total = real[freq : freq + 1, :]
            scale = lax.rsqrt(total * jnp.float32(freq))
            even = apply(cos_both, cos_high, real) * scale
            odd = apply(sin_both, sin_high, imag) * scale
            later = even - odd
            earlier = even + odd
            for k in range(HALF + 1):
                out[r, HALF + k, a : a + 1, :] = later[k : k + 1]
            for k in range(1, HALF + 1):
                out[r, HALF - k, a : a + 1, :] = earlier[k : k + 1]


def on_device(spectra, match, counts):
    slots, parts, freq, block = spectra.shape
    chans = lax.axis_size("chan")
    bins = chans * lax.axis_size("seg")
    tile = slots * parts

    valid = (jnp.arange(slots, dtype=jnp.int32) < counts[0]).astype(jnp.bfloat16)
    own = spectra * valid[:, None, None, None]
    own = jnp.transpose(own, (2, 1, 0, 3)).reshape(freq, tile, block)
    ones = jnp.concatenate([valid, jnp.zeros_like(valid)])
    ones = jnp.broadcast_to(ones[None, :, None], (1, tile, block))
    rest = jnp.zeros((bins - freq - 1, tile, block), jnp.bfloat16)
    send = jnp.concatenate([own, ones, rest], axis=0)

    here = lax.all_to_all(send, ("chan", "seg"), 0, 0, tiled=True)
    here = here.reshape(chans, bins // chans * tile, block)

    rows = ROUNDS * tile
    cross = pl.pallas_call(
        cross_kernel,
        out_shape=jax.ShapeDtypeStruct((bins, rows, block), jnp.float32),
        in_specs=[
            pl.BlockSpec(memory_space=pltpu.SMEM),
            pl.BlockSpec(memory_space=pltpu.VMEM),
        ],
        out_specs=pl.BlockSpec(memory_space=pltpu.VMEM),
        scratch_shapes=[pltpu.VMEM((chans, 2 * block, 2 * block), jnp.bfloat16)],
        compiler_params=pltpu.CompilerParams(vmem_limit_bytes=24 * 1024 * 1024),
        name="cross",
    )(match, here)

    mine = lax.all_to_all(cross, ("chan", "seg"), 0, 0, tiled=True)
    mine = mine.reshape(bins * rows, block)

    cos, sin = tables(freq, bins)
    return pl.pallas_call(
        lambda *refs: lag_kernel(freq, *refs),
        out_shape=jax.ShapeDtypeStruct((ROUNDS, LAGS, tile // 2, block), jnp.float32),
        in_specs=[pl.BlockSpec(memory_space=pltpu.VMEM)] * 3,
        out_specs=pl.BlockSpec(memory_space=pltpu.VMEM),
        compiler_params=pltpu.CompilerParams(vmem_limit_bytes=24 * 1024 * 1024),
        name="lags",
    )(jnp.asarray(cos), jnp.asarray(sin), mine)


def solution(mesh):
    return jax.shard_map(
        on_device,
        mesh=mesh,
        in_specs=(P("seg", None, None, "chan"), P(), P("seg")),
        out_specs=P(None, None, ("chan", "seg"), None),
        check_vma=False,
    )
```

time: 535 us -> 129 us (0.24); the launches traced: 526 us -> 128 us
  waiting for transfers between devices: 269 us -> 0 us
  matrix products: 141 us -> 0 us
  blocking collectives: 53.9 us -> 119 us
  other arithmetic: 41.6 us -> 1.28 us
  between operations: 16.7 us -> 0.73 us
  Pallas kernels: 0 us -> 6.33 us
    reduce_scatter x3 -> x0, waiting for transfers between devices: 182 us -> none  [on_device(): lax.psum_scatter(lagged, 'seg', scatter_dimension=1, tiled=True)]
    dot_general x9 -> x0, matrix products: 141 us -> none  [the longest x3 124 us: on_device(): jnp.dot(table, both, precision=lax.Precision.HIGHEST)]
    all_to_all x0 -> x2, blocking collectives: none -> 119 us  [the longest x1 82.6 us: on_device(): mine = lax.all_to_all(cross, ('chan', 'seg'), 0, 0, tiled=True)]
    all_gather x1 -> x0, waiting for transfers between devices: 86.9 us -> none  [on_device(): whole = lax.all_gather(spectra, 'chan', axis=3, tiled=True)]
    psum x1 -> x0, blocking collectives: 53.9 us -> none  [on_device(): total = lax.psum(jnp.sum(counts).astype(jnp.float32), 'seg')]
    concatenate x3 -> x1, other arithmetic: 37.3 us -> 0.18 us  [on_device(): send = jnp.concatenate([own, ones, rest], axis=0)]
    pallas_call x0 -> x2, Pallas kernels: none -> 6.33 us  [the longest x1 4.53 us: on_device(): pl.pallas_call(cross_kernel, out_shape=jax.ShapeDtypeStruct((bins, rows,...]
  transfers between devices with their start and end apart: 4 -> 0, of which waited for: 3 -> 0; matrix products, arithmetic and copies ran while one was open for 23% -> 0% of each run, Pallas kernels for 0% -> 0%
where the time goes in v1:
time: 129 us; the launch traced here: 128 us
  blocking collectives  119 us (92%)
  Pallas kernels  6.33 us (5%)
    all_to_all x1, blocking collectives, on_device(): mine = lax.all_to_all(cross, ('chan', 'seg'), 0, 0, tiled=True)  82.6 us
    all_to_all x1, blocking collectives, on_device(): here = lax.all_to_all(send, ('chan', 'seg'), 0, 0, tiled=True)  36.9 us
    pallas_call x1, Pallas kernels, on_device(): pl.pallas_call(cross_kernel, out_shape=jax.ShapeDtypeStruct((bins, rows,...  4.53 us

profile of v1, /device:TPU:1, one launch (start us, length us, event | category | flops | bytes accessed | tf_op | source)
XLA Modules:
  0.0 128.3 jit_solution(11259205355759343509)
XLA Ops:
  0.0 0.0 copy-start.2
  0.7 1.1 copy_multiply_fusion
  1.8 0.1 pad.3.clone
  1.9 0.1 broadcast_in_dim.4
  2.0 0.2 maximum_maximum_fusion
  2.1 0.3 copy.9
  2.5 36.9 %all_to_all.10 = bf16[256,8,128]{2,1,0:T(8,128)(2,1)S(1)} all-to-all(bf16[256,8,128]{2,1,0:T(8,128)(2,1)S(1)} %copy.9), channel_id=1, replica_groups=mesh['chan'=8,'seg'=32] {'chan','seg'}, dimensions={0} | all-to-all | bytes 1048576 | tf_op jit(solution)/shard_map/all_to_all | solution.py:111
  39.4 0.0 copy-done.2
  39.4 4.5 %cross.1 = f32[256,24,128]{2,1,0:T(8,128)S(1)} custom-call(s32[3,8]{1,0:T(4,128)S(1)} %copy-done.2, bf16[8,256,128]{2,1,0:T(8,128)(2,1)S(1)} %bitcast.8), custom_call_target="tpu_custom_call" | custom-call | tf_op jit(solution)/shard_map/cross/pallas_call | solution.py:115
  43.9 0.0 copy-start
  43.9 0.0 copy-start.1
  43.9 82.6 %all_to_all.11 = f32[256,24,128]{2,1,0:T(8,128)S(1)} all-to-all(f32[256,24,128]{2,1,0:T(8,128)S(1)} %cross.1), channel_id=1, replica_groups=mesh['chan'=8,'seg'=32] {'chan','seg'}, dimensions={0} | all-to-all | bytes 6291456 | tf_op jit(solution)/shard_map/all_to_all | solution.py:128
  126.5 0.0 copy-done
  126.5 0.0 copy-done.1
  126.5 1.8 %lags.1 = f32[3,51,4,128]{3,2,1,0:T(4,128)} custom-call(f32[32,256]{1,0:T(8,128)S(1)} %copy-done.1, f32[32,256]{1,0:T(8,128)S(1)} %copy-done, f32[6144,128]{1,0:T(8,128)S(1)} %bitcast.7), custom_call_target="tpu_custom_call" | custom-call | tf_op jit(solution)/shard_map/lags/pallas_call | solution.py:132
  (3 shorter events, 0.0 us)
Async XLA Ops:
  0.0 39.4 %copy-start.2 = (s32[3,8]{1,0:T(4,128)S(1)}, s32[3,8]{1,0:T(4,128)}, u32[]{:S(2)}) copy-start(s32[3,8]{1,0:T(4,128)} %match.1) | copy-start | bytes 292
  43.9 82.6 %copy-start = (f32[32,256]{1,0:T(8,128)S(1)}, f32[32,256]{1,0:T(8,128)}, u32[]{:S(2)}) copy-start(f32[32,256]{1,0:T(8,128)} %constant.8.clone.refs_1_) | copy-start | bytes 98308
  43.9 82.6 %copy-start.1 = (f32[32,256]{1,0:T(8,128)S(1)}, f32[32,256]{1,0:T(8,128)}, u32[]{:S(2)}) copy-start(f32[32,256]{1,0:T(8,128)} %constant.2.clone.refs_0_) | copy-start | bytes 98308

commit v2 on v1

v2 whole, which is shorter than its diff:
```python
import functools

import jax
import jax.numpy as jnp
import numpy as np
from jax import lax
from jax.experimental import pallas as pl
from jax.experimental.pallas import tpu as pltpu
from jax.sharding import PartitionSpec as P

LAGS = 51
SAMPLES = 3000
ROUNDS = 3
HALF = LAGS // 2
ROWS = 32
LANES = 128

KNEE = 2.0**-10
TOP = 32000.0
UNIT = 8192.0


def tables(freq, bins):
    lag = np.arange(ROWS, dtype=np.float64)[:, None]
    f = np.arange(bins, dtype=np.float64)[None, :] + 1.0
    angle = 2.0 * np.pi * f * lag / SAMPLES
    live = (np.arange(bins)[None, :] < freq) & (np.arange(ROWS)[:, None] <= HALF)
    return (
        np.where(live, np.cos(angle), 0.0).astype(np.float32),
        np.where(live, np.sin(angle), 0.0).astype(np.float32),
    )


def per_octave(depth):
    return TOP / float(np.log2(1.0 + depth / KNEE))


def send_kernel(counts, x, out, rows):
    slots, parts, freq, block = x.shape
    bins, tile, _ = out.shape
    rows[freq * tile :, :] = jnp.zeros(((bins - freq) * tile, block), jnp.float32)
    peak = jnp.zeros((freq, block), jnp.float32)
    for s in range(slots):
        valid = (s < counts[0]).astype(jnp.float32)
        for p in range(parts):
            at = p * slots + s
            v = x[s, p].astype(jnp.float32) * valid
            rows[pl.ds(at, freq, stride=tile), :] = v
            peak = jnp.maximum(peak, jnp.abs(v))
        rows[freq * tile + s : freq * tile + s + 1, :] = jnp.full((1, block), valid, jnp.float32)
    peak = jnp.concatenate([peak, jnp.zeros((2 * LANES - freq, block), jnp.float32)], axis=0)
    for i in range(2):
        row = (freq + 1) * tile + i
        part = jnp.transpose(peak[i * LANES : (i + 1) * LANES, :])
        rows[row : row + 1, :] = jnp.max(part, axis=0, keepdims=True)
    out[...] = rows[...].astype(jnp.bfloat16).reshape(out.shape)


def cross_kernel(freq, place, match, x, out, order, peak):
    blocks, depth, block = x.shape
    sources, rows, _ = out.shape
    tile = rows // ROUNDS
    half = tile // 2
    c = pl.program_id(0)

    @pl.when(c == 0)
    def _():
        row = lax.broadcasted_iota(jnp.int32, (2 * block, 2 * block), 0)
        col = lax.broadcasted_iota(jnp.int32, (2 * block, 2 * block), 1)
        channel = (row // tile) * half + row % half
        part = (row % tile) // half
        order[...] = (col == part * block + channel).astype(jnp.bfloat16)
        peak[0] = jnp.max(jnp.abs(x[...].astype(jnp.float32)))

    most = peak[0]
    inverse = jnp.where(most > 0.0, 1.0 / jnp.maximum(most, 1e-37), 0.0)

    own = x[c]
    groups = own.astype(jnp.float32).reshape(sources, tile, block)
    swapped = jnp.concatenate([groups[:, half:], -groups[:, :half]], axis=1)
    both = jnp.concatenate([own, swapped.reshape(depth, block).astype(jnp.bfloat16)], axis=1)
    turned = lax.dot_general(
        order[...], both, (((1,), (1,)), ((), ())), preferred_element_type=jnp.float32
    ).astype(jnp.bfloat16)
    coded = []
    for r in range(ROUNDS):
        product = jnp.dot(turned, x[match[r, c]], preferred_element_type=jnp.float32)
        y = product * inverse * inverse
        code = jnp.log2(1.0 + jnp.abs(y) * (1.0 / KNEE)) * per_octave(depth)
        code = jnp.round(jnp.where(y < 0.0, -code, code))
        coded.append(code.astype(jnp.int32).astype(jnp.int16).reshape(sources, tile, block))
    out[...] = jnp.concatenate(coded, axis=1)

    @pl.when(place[0] == freq + 1)
    def _():
        most = jnp.max(x[...].astype(jnp.float32).reshape(blocks * sources, tile, block), axis=0)
        power = jnp.floor(jnp.log2(jnp.maximum(most, 1e-37)))
        share = jnp.round(most * jnp.exp2(-power) * UNIT)
        rest = jnp.zeros(((ROUNDS - 2) * tile, block), jnp.float32)
        both = jnp.concatenate([power, share, rest], axis=0).astype(jnp.int32).astype(jnp.int16)
        out[...] = jnp.broadcast_to(both[None], out.shape)


def split(v):
    high = v.astype(jnp.bfloat16)
    return high, (v - high.astype(jnp.float32)).astype(jnp.bfloat16)


def lag_kernel(freq, depth, cos, sin, coded, out, x):
    bins = cos.shape[1]
    rows = coded.shape[1]
    tile = rows // ROUNDS
    half = tile // 2
    x[...] = coded[...].astype(jnp.int32).reshape(x.shape)

    at = (freq + 1) * rows
    power = x[at : at + tile, :].astype(jnp.float32)
    share = x[at + tile : at + 2 * tile, :].astype(jnp.float32)
    most = share * jnp.exp2(power) * (1.0 / UNIT)
    most = jnp.concatenate([most[i : i + 1] for i in range(bins // LANES)], axis=1)

    def both(table):
        high, low = split(table[...] * most * most * KNEE)
        return jnp.concatenate([high, low], axis=0), high

    def apply(tables, v):
        high, low = split(v)
        first = jnp.dot(tables[0], high, preferred_element_type=jnp.float32)
        return first[:ROWS] + first[ROWS:] + jnp.dot(tables[1], low, preferred_element_type=jnp.float32)

    def load(at):
        code = x[pl.ds(at, bins, stride=rows), :].astype(jnp.float32)
        size = jnp.exp2(jnp.abs(code) * (1.0 / per_octave(depth))) - 1.0
        return jnp.where(code < 0.0, -size, size)

    cos = both(cos)
    sin = both(sin)
    for r in range(ROUNDS):
        for a in range(half):
            real = load(r * tile + a)
            imag = load(r * tile + a + half)
            total = jnp.round(real[freq : freq + 1, :] * KNEE)
            scale = lax.rsqrt(total * jnp.float32(freq))
            even = apply(cos, real) * scale
            odd = apply(sin, imag) * scale
            later = even - odd
            earlier = even + odd
            for k in range(HALF + 1):
                out[r, HALF + k, a : a + 1, :] = later[k : k + 1]
            for k in range(1, HALF + 1):
                out[r, HALF - k, a : a + 1, :] = earlier[k : k + 1]


def on_device(spectra, match, counts):
    slots, parts, freq, block = spectra.shape
    chans = lax.axis_size("chan")
    segs = lax.axis_size("seg")
    bins = chans * segs
    tile = slots * parts
    depth = segs * tile
    rows = ROUNDS * tile
    place = lax.axis_index("chan") * segs + lax.axis_index("seg")

    vmem = pl.BlockSpec(memory_space=pltpu.VMEM)
    smem = pl.BlockSpec(memory_space=pltpu.SMEM)
    params = pltpu.CompilerParams(vmem_limit_bytes=24 * 1024 * 1024)

    send = pl.pallas_call(
        send_kernel,
        out_shape=jax.ShapeDtypeStruct((bins, tile, block), jnp.bfloat16),
        in_specs=[smem, vmem],
        out_specs=vmem,
        scratch_shapes=[pltpu.VMEM((bins * tile, block), jnp.float32)],
        compiler_params=params,
        name="send",
    )(counts, spectra)

    here = lax.all_to_all(send, ("chan", "seg"), 0, 0, tiled=True)
    here = here.reshape(chans, depth, block)

    cross = pl.pallas_call(
        functools.partial(cross_kernel, freq),
        grid=(chans,),
        out_shape=jax.ShapeDtypeStruct((bins, rows, block), jnp.int16),
        in_specs=[smem, smem, vmem],
        out_specs=pl.BlockSpec((segs, rows, block), lambda c: (c, 0, 0)),
        scratch_shapes=[
            pltpu.VMEM((2 * block, 2 * block), jnp.bfloat16),
            pltpu.SMEM((1,), jnp.float32),
        ],
        compiler_params=params,
        name="cross",
    )(place.astype(jnp.int32).reshape(1), match, here)

    mine = lax.all_to_all(cross, ("chan", "seg"), 0, 0, tiled=True)

    cos, sin = tables(freq, bins)
    return pl.pallas_call(
        functools.partial(lag_kernel, freq, depth),
        out_shape=jax.ShapeDtypeStruct((ROUNDS, LAGS, tile // 2, block), jnp.float32),
        in_specs=[vmem] * 3,
        out_specs=vmem,
        scratch_shapes=[pltpu.VMEM((bins * rows, block), jnp.int32)],
        compiler_params=params,
        name="lags",
    )(jnp.asarray(cos), jnp.asarray(sin), mine)


def solution(mesh):
    return jax.shard_map(
        on_device,
        mesh=mesh,
        in_specs=(P("seg", None, None, "chan"), P(), P("seg")),
        out_specs=P(None, None, ("chan", "seg"), None),
        check_vma=False,
    )
```

time: 129 us -> 97.1 us (0.75)
  blocking collectives: 119 us -> 49.3 us
  waiting for transfers between devices: 0 us -> 21.4 us
  starting transfers between devices: 0 us -> 15.7 us
  Pallas kernels: 6.33 us -> 8.75 us
    all_to_all x1 -> x0, blocking collectives: 36.9 us -> none  [on_device(): here = lax.all_to_all(send, ('chan', 'seg'), 0, 0, tiled=True)]
    all_to_all x1, blocking collectives: 82.6 us -> 49.3 us  [on_device(): mine = lax.all_to_all(cross, ('chan', 'seg'), 0, 0, tiled=True)]
    all_to_all x0 -> x1, waiting for transfers between devices: none -> 21.4 us  [on_device(): here = lax.all_to_all(send, ('chan', 'seg'), 0, 0, tiled=True)]
    all_to_all x0 -> x1, starting transfers between devices: none -> 15.7 us  [on_device(): here = lax.all_to_all(send, ('chan', 'seg'), 0, 0, tiled=True)]
    pallas_call x2 -> x3, Pallas kernels: 6.33 us -> 8.75 us  [the longest x1 5.1 us: on_device(): pl.pallas_call(functools.partial(cross_kernel, freq), grid=(chans,), out_...]
  transfers between devices with their start and end apart: 0 -> 1, of which waited for: 0 -> 1; matrix products, arithmetic and copies ran while one was open for 0% -> 0% of each run, Pallas kernels for 0% -> 0%
where the time goes in v2:
time: 97.1 us; the launch traced here: 96.8 us
  blocking collectives  49.3 us (51%)
  waiting for transfers between devices  21.4 us (22%)
  starting transfers between devices  15.7 us (16%)
  Pallas kernels  8.75 us (9%)
  local copies, waits for them, and re-layouts  1.01 us (1%)
    all_to_all x1, blocking collectives, on_device(): mine = lax.all_to_all(cross, ('chan', 'seg'), 0, 0, tiled=True)  49.3 us
    all_to_all x1, waiting for transfers between devices, on_device(): here = lax.all_to_all(send, ('chan', 'seg'), 0, 0, tiled=True)  21.4 us
    all_to_all x1, starting transfers between devices, on_device(): here = lax.all_to_all(send, ('chan', 'seg'), 0, 0, tiled=True)  15.7 us
    pallas_call x1, Pallas kernels, on_device(): pl.pallas_call(functools.partial(cross_kernel, freq), grid=(chans,), out_...  5.1 us
    pallas_call x1, Pallas kernels, on_device(): pl.pallas_call(functools.partial(lag_kernel, freq, depth), out_shape=jax....  2.56 us
  transfers between devices with their start and end apart: 1, of which 1 were waited for; matrix products, arithmetic and copies ran while one was open for 0% of the time, Pallas kernels for 0%

profile of v2, /device:TPU:1, one launch (start us, length us, event | category | flops | bytes accessed | tf_op | source)
XLA Modules:
  0.0 96.8 jit_solution(214880944829813267)
XLA Ops:
  0.7 0.0 copy-start
  0.7 1.0 %copy-done = bf16[4,2,200,128]{3,2,1,0:T(8,128)(2,1)S(1)} copy-done((bf16[4,2,200,128]{3,2,1,0:T(8,128)(2,1)S(1)}, bf16[4,2,200,128]{3,2,1,0:T(8,128)(2,1)}, u32[]{:S(2)}) %copy-start) | copy-done | bytes 409624
  1.7 0.0 copy-start.3
  1.7 1.1 %send.1 = bf16[256,8,128]{2,1,0:T(8,128)(2,1)} custom-call(s32[1]{0:T(128)S(6)} %copy.6.counts, bf16[4,2,200,128]{3,2,1,0:T(8,128)(2,1)S(1)} %copy-done), custom_call_target="tpu_custom_call" | custom-call | tf_op jit(solution)/shard_map/send/pallas_call | solution.py:168
  2.7 15.7 %all-to-all-start = ((bf16[256,8,128]{2,1,0:T(8,128)(2,1)}), bf16[256,8,128]{2,1,0:T(8,128)(2,1)S(1)}, u32[]{:S(2)}, u32[]{:S(2)}) async-start(bf16[256,8,128]{2,1,0:T(8,128)(2,1)} %send.1), calls=%async_computation | async-start | bytes 1048576 | tf_op jit(solution)/shard_map/all_to_all | solution.py:178
  18.4 21.4 %all-to-all-done = bf16[256,8,128]{2,1,0:T(8,128)(2,1)S(1)} async-done(((bf16[256,8,128]{2,1,0:T(8,128)(2,1)}), bf16[256,8,128]{2,1,0:T(8,128)(2,1)S(1)}, u32[]{:S(2)}, u32[]{:S(2)}) %all-to-all-start) | async-done | bytes 524320 | tf_op jit(solution)/shard_map/all_to_all | solution.py:178
  39.8 0.0 copy-done.3
  39.8 5.1 %cross.1 = s16[256,24,128]{2,1,0:T(8,128)(2,1)S(1)} custom-call(s32[1]{0:T(128)} %bitcast.place, s32[3,8]{1,0:T(4,128)S(1)} %copy-done.3, bf16[8,256,128]{2,1,0:T(8,128)(2,1)S(1)} %bitcast.2), custom_call_target="tpu_custom_call" | custom-call | tf_op jit(solution)/shard_map/cross/pallas_call | solution.py:181
  44.9 0.0 copy-start.1
  45.0 0.0 copy-start.2
  45.0 49.3 %all_to_all.10.coded = s16[256,24,128]{2,1,0:T(8,128)(2,1)S(1)} all-to-all(s16[256,24,128]{2,1,0:T(8,128)(2,1)S(1)} %cross.1), channel_id=1, replica_groups=mesh['chan'=8,'seg'=32] {'chan','seg'}, dimensions={0} | all-to-all | bytes 3145728 | tf_op jit(solution)/shard_map/all_to_all | solution.py:195
  94.2 0.0 copy-done.1
  94.2 0.0 copy-done.2
  94.2 2.6 %lags.1 = f32[3,51,4,128]{3,2,1,0:T(4,128)} custom-call(f32[32,256]{1,0:T(8,128)S(1)} %copy-done.2, f32[32,256]{1,0:T(8,128)S(1)} %copy-done.1, s16[256,24,128]{2,1,0:T(8,128)(2,1)S(1)} %all_to_all.10.coded), custom_call_target="tpu_custom_call" | custom-call | tf_op jit(solution)/shard_map/lags/pallas_call | solution.py:198
Async XLA Ops:
  0.7 1.0 %copy-start = (bf16[4,2,200,128]{3,2,1,0:T(8,128)(2,1)S(1)}, bf16[4,2,200,128]{3,2,1,0:T(8,128)(2,1)}, u32[]{:S(2)}) copy-start(bf16[4,2,200,128]{3,2,1,0:T(8,128)(2,1)} %x.1) | copy-start | bytes 1228804
  1.7 38.2 %copy-start.3 = (s32[3,8]{1,0:T(4,128)S(1)}, s32[3,8]{1,0:T(4,128)}, u32[]{:S(2)}) copy-start(s32[3,8]{1,0:T(4,128)} %match.1) | copy-start | bytes 292
  2.7 37.1 %all-to-all-start = ((bf16[256,8,128]{2,1,0:T(8,128)(2,1)}), bf16[256,8,128]{2,1,0:T(8,128)(2,1)S(1)}, u32[]{:S(2)}, u32[]{:S(2)}) async-start(bf16[256,8,128]{2,1,0:T(8,128)(2,1)} %send.1), calls=%async_computation | async-start | bytes 1048576 | tf_op jit(solution)/shard_map/all_to_all | solution.py:178
  44.9 49.3 %copy-start.1 = (f32[32,256]{1,0:T(8,128)S(1)}, f32[32,256]{1,0:T(8,128)}, u32[]{:S(2)}) copy-start(f32[32,256]{1,0:T(8,128)} %constant.16.clone.sin) | copy-start | bytes 98308
  45.0 49.3 %copy-start.2 = (f32[32,256]{1,0:T(8,128)S(1)}, f32[32,256]{1,0:T(8,128)}, u32[]{:S(2)}) copy-start(f32[32,256]{1,0:T(8,128)} %constant.15.clone.cos) | copy-start | bytes 98308

commit v3 on v2

--- a/solution.py
+++ b/solution.py
@@ -31,8 +31,8 @@
     )
 
 
-def per_octave(depth):
-    return TOP / float(np.log2(1.0 + depth / KNEE))
+def per_e(depth):
+    return TOP / float(np.log(1.0 + depth / KNEE))
 
 
 def send_kernel(counts, x, out, rows):
@@ -56,40 +56,40 @@
     out[...] = rows[...].astype(jnp.bfloat16).reshape(out.shape)
 
 
-def cross_kernel(freq, place, match, x, out, order, peak):
+def cross_kernel(freq, place, match, x, out):
     blocks, depth, block = x.shape
-    sources, rows, _ = out.shape
+    bins, rows, _ = out.shape
+    sources = bins // blocks
     tile = rows // ROUNDS
     half = tile // 2
-    c = pl.program_id(0)
-
-    @pl.when(c == 0)
-    def _():
-        row = lax.broadcasted_iota(jnp.int32, (2 * block, 2 * block), 0)
-        col = lax.broadcasted_iota(jnp.int32, (2 * block, 2 * block), 1)
-        channel = (row // tile) * half + row % half
-        part = (row % tile) // half
-        order[...] = (col == part * block + channel).astype(jnp.bfloat16)
-        peak[0] = jnp.max(jnp.abs(x[...].astype(jnp.float32)))
-
-    most = peak[0]
+
+    row = lax.broadcasted_iota(jnp.int32, (2 * block, 2 * block), 0)
+    col = lax.broadcasted_iota(jnp.int32, (2 * block, 2 * block), 1)
+    channel = (row // tile) * half + row % half
+    part = (row % tile) // half
+    order = (col == part * block + channel).astype(jnp.bfloat16)
+    most = jnp.max(jnp.abs(x[...].astype(jnp.float32)))
     inverse = jnp.where(most > 0.0, 1.0 / jnp.maximum(most, 1e-37), 0.0)
 
-    own = x[c]
-    groups = own.astype(jnp.float32).reshape(sources, tile, block)
-    swapped = jnp.concatenate([groups[:, half:], -groups[:, :half]], axis=1)
-    both = jnp.concatenate([own, swapped.reshape(depth, block).astype(jnp.bfloat16)], axis=1)
-    turned = lax.dot_general(
-        order[...], both, (((1,), (1,)), ((), ())), preferred_element_type=jnp.float32
-    ).astype(jnp.bfloat16)
-    coded = []
-    for r in range(ROUNDS):
-        product = jnp.dot(turned, x[match[r, c]], preferred_element_type=jnp.float32)
-        y = product * inverse * inverse
-        code = jnp.log2(1.0 + jnp.abs(y) * (1.0 / KNEE)) * per_octave(depth)
-        code = jnp.round(jnp.where(y < 0.0, -code, code))
-        coded.append(code.astype(jnp.int32).astype(jnp.int16).reshape(sources, tile, block))
-    out[...] = jnp.concatenate(coded, axis=1)
+    def one(c):
+        own = x[c]
+        groups = own.astype(jnp.float32).reshape(sources, tile, block)
+        swapped = jnp.concatenate([groups[:, half:], -groups[:, :half]], axis=1)
+        both = jnp.concatenate([own, swapped.reshape(depth, block).astype(jnp.bfloat16)], axis=1)
+        turned = lax.dot_general(
+            order, both, (((1,), (1,)), ((), ())), preferred_element_type=jnp.float32
+        ).astype(jnp.bfloat16)
+        coded = []
+        for r in range(ROUNDS):
+            product = jnp.dot(turned, x[match[r, c]], preferred_element_type=jnp.float32)
+            y = product * (inverse * (1.0 / KNEE)) * inverse
+            code = (jnp.log(1.0 + jnp.abs(y)) * per_e(depth) + 0.5).astype(jnp.int32)
+            code = jnp.where(y < 0.0, -code, code)
+            coded.append(code.astype(jnp.int16).reshape(sources, tile, block))
+        out[pl.ds(c * sources, sources)] = jnp.concatenate(coded, axis=1)
+
+    for c in range(blocks):
+        one(c)
 
     @pl.when(place[0] == freq + 1)
     def _():
@@ -130,36 +130,34 @@
 
     def load(at):
         code = x[pl.ds(at, bins, stride=rows), :].astype(jnp.float32)
-        size = jnp.exp2(jnp.abs(code) * (1.0 / per_octave(depth))) - 1.0
+        size = jnp.exp(jnp.abs(code) * (1.0 / per_e(depth))) - 1.0
         return jnp.where(code < 0.0, -size, size)
 
     cos = both(cos)
     sin = both(sin)
     for r in range(ROUNDS):
-        for a in range(half):
-            real = load(r * tile + a)
-            imag = load(r * tile + a + half)
+        for a in range(0, half, 2):
+            real = jnp.concatenate([load(r * tile + a), load(r * tile + a + 1)], axis=1)
+            imag = jnp.concatenate([load(r * tile + a + half), load(r * tile + a + 1 + half)], axis=1)
             total = jnp.round(real[freq : freq + 1, :] * KNEE)
             scale = lax.rsqrt(total * jnp.float32(freq))
             even = apply(cos, real) * scale
             odd = apply(sin, imag) * scale
             later = even - odd
             earlier = even + odd
-            for k in range(HALF + 1):
-                out[r, HALF + k, a : a + 1, :] = later[k : k + 1]
-            for k in range(1, HALF + 1):
-                out[r, HALF - k, a : a + 1, :] = earlier[k : k + 1]
-
-
-def on_device(spectra, match, counts):
-    slots, parts, freq, block = spectra.shape
-    chans = lax.axis_size("chan")
-    segs = lax.axis_size("seg")
+            for i in range(2):
+                at = slice(i * LANES, (i + 1) * LANES)
+                for k in range(HALF + 1):
+                    out[r, HALF + k, a + i : a + i + 1, :] = later[k : k + 1, at]
+                for k in range(1, HALF + 1):
+                    out[r, HALF - k, a + i : a + i + 1, :] = earlier[k : k + 1, at]
+
+
+def kernels(slots, parts, freq, block, chans, segs):
     bins = chans * segs
     tile = slots * parts
     depth = segs * tile
     rows = ROUNDS * tile
-    place = lax.axis_index("chan") * segs + lax.axis_index("seg")
 
     vmem = pl.BlockSpec(memory_space=pltpu.VMEM)
     smem = pl.BlockSpec(memory_space=pltpu.SMEM)
@@ -173,29 +171,16 @@
         scratch_shapes=[pltpu.VMEM((bins * tile, block), jnp.float32)],
         compiler_params=params,
         name="send",
-    )(counts, spectra)
-
-    here = lax.all_to_all(send, ("chan", "seg"), 0, 0, tiled=True)
-    here = here.reshape(chans, depth, block)
-
+    )
     cross = pl.pallas_call(
         functools.partial(cross_kernel, freq),
-        grid=(chans,),
         out_shape=jax.ShapeDtypeStruct((bins, rows, block), jnp.int16),
         in_specs=[smem, smem, vmem],
-        out_specs=pl.BlockSpec((segs, rows, block), lambda c: (c, 0, 0)),
-        scratch_shapes=[
-            pltpu.VMEM((2 * block, 2 * block), jnp.bfloat16),
-            pltpu.SMEM((1,), jnp.float32),
-        ],
+        out_specs=vmem,
         compiler_params=params,
         name="cross",
-    )(place.astype(jnp.int32).reshape(1), match, here)
-
-    mine = lax.all_to_all(cross, ("chan", "seg"), 0, 0, tiled=True)
-
-    cos, sin = tables(freq, bins)
-    return pl.pallas_call(
+    )
+    lags = pl.pallas_call(
         functools.partial(lag_kernel, freq, depth),
         out_shape=jax.ShapeDtypeStruct((ROUNDS, LAGS, tile // 2, block), jnp.float32),
         in_specs=[vmem] * 3,
@@ -203,7 +188,22 @@
         scratch_shapes=[pltpu.VMEM((bins * rows, block), jnp.int32)],
         compiler_params=params,
         name="lags",
-    )(jnp.asarray(cos), jnp.asarray(sin), mine)
+    )
+    cos, sin = tables(freq, bins)
+    return send, cross, functools.partial(lags, jnp.asarray(cos), jnp.asarray(sin))
+
+
+def on_device(spectra, match, counts):
+    slots, parts, freq, block = spectra.shape
+    chans = lax.axis_size("chan")
+    segs = lax.axis_size("seg")
+    place = lax.axis_index("chan") * segs + lax.axis_index("seg")
+    send, cross, lags = kernels(slots, parts, freq, block, chans, segs)
+
+    here = lax.all_to_all(send(counts, spectra), ("chan", "seg"), 0, 0, tiled=True)
+    here = here.reshape(chans, segs * slots * parts, block)
+    coded = cross(place.astype(jnp.int32).reshape(1), match, here)
+    return lags(lax.all_to_all(coded, ("chan", "seg"), 0, 0, tiled=True))
 
 
 def solution(mesh):

time: 97.1 us -> 95 us (0.978)
  Pallas kernels: 8.75 us -> 6.9 us
    pallas_call x3, Pallas kernels: 8.75 us -> 6.9 us  [the longest x1 3.2 us: on_device(): coded = cross(place.astype(jnp.int32).reshape(1), match, here)]
where the time goes in v3:
time: 95 us; the launch traced here: 94.7 us
  blocking collectives  49 us (52%)
  waiting for transfers between devices  21.4 us (23%)
  starting transfers between devices  15.7 us (17%)
  Pallas kernels  6.9 us (7%)
  local copies, waits for them, and re-layouts  1.01 us (1%)
    all_to_all x1, blocking collectives, on_device(): return lags(lax.all_to_all(coded, ('chan', 'seg'), 0, 0, tiled=True))  49 us
    all_to_all x1, waiting for transfers between devices, on_device(): lax.all_to_all(send(counts, spectra), ('chan', 'seg'), 0, 0, tiled=True)  21.4 us
    all_to_all x1, starting transfers between devices, on_device(): lax.all_to_all(send(counts, spectra), ('chan', 'seg'), 0, 0, tiled=True)  15.7 us
    pallas_call x1, Pallas kernels, on_device(): coded = cross(place.astype(jnp.int32).reshape(1), match, here)  3.2 us
    pallas_call x1, Pallas kernels, on_device(): return lags(lax.all_to_all(coded, ('chan', 'seg'), 0, 0, tiled=True))  2.62 us
  transfers between devices with their start and end apart: 1, of which 1 were waited for; matrix products, arithmetic and copies ran while one was open for 0% of the time, Pallas kernels for 0%

profile of v3, /device:TPU:1, one launch (start us, length us, event | category | flops | bytes accessed | tf_op | source)
XLA Modules:
  0.0 94.7 jit_solution(4701290420609132520)
XLA Ops:
  0.7 0.0 copy-start
  0.7 1.0 %copy-done = bf16[4,2,200,128]{3,2,1,0:T(8,128)(2,1)S(1)} copy-done((bf16[4,2,200,128]{3,2,1,0:T(8,128)(2,1)S(1)}, bf16[4,2,200,128]{3,2,1,0:T(8,128)(2,1)}, u32[]{:S(2)}) %copy-start) | copy-done | bytes 409624
  1.7 0.0 copy-start.3
  1.7 1.1 %send.1 = bf16[256,8,128]{2,1,0:T(8,128)(2,1)} custom-call(s32[1]{0:T(128)S(6)} %copy.6.counts, bf16[4,2,200,128]{3,2,1,0:T(8,128)(2,1)S(1)} %copy-done), custom_call_target="tpu_custom_call" | custom-call | tf_op jit(solution)/shard_map/send/pallas_call | solution.py:203
  2.7 15.7 %all-to-all-start = ((bf16[256,8,128]{2,1,0:T(8,128)(2,1)}), bf16[256,8,128]{2,1,0:T(8,128)(2,1)S(1)}, u32[]{:S(2)}, u32[]{:S(2)}) async-start(bf16[256,8,128]{2,1,0:T(8,128)(2,1)} %send.1), calls=%async_computation | async-start | bytes 1048576 | tf_op jit(solution)/shard_map/all_to_all | solution.py:203
  18.4 21.4 %all-to-all-done = bf16[256,8,128]{2,1,0:T(8,128)(2,1)S(1)} async-done(((bf16[256,8,128]{2,1,0:T(8,128)(2,1)}), bf16[256,8,128]{2,1,0:T(8,128)(2,1)S(1)}, u32[]{:S(2)}, u32[]{:S(2)}) %all-to-all-start) | async-done | bytes 524320 | tf_op jit(solution)/shard_map/all_to_all | solution.py:203
  39.8 0.0 copy-done.3
  39.8 3.2 %cross.1 = s16[256,24,128]{2,1,0:T(8,128)(2,1)S(1)} custom-call(s32[1]{0:T(128)} %bitcast.place, s32[3,8]{1,0:T(4,128)S(1)} %copy-done.3, bf16[8,256,128]{2,1,0:T(8,128)(2,1)S(1)} %bitcast.2), custom_call_target="tpu_custom_call" | custom-call | tf_op jit(solution)/shard_map/cross/pallas_call | solution.py:205
  43.0 0.0 copy-start.1
  43.1 0.0 copy-start.2
  43.1 49.0 %all_to_all.10.coded = s16[256,24,128]{2,1,0:T(8,128)(2,1)S(1)} all-to-all(s16[256,24,128]{2,1,0:T(8,128)(2,1)S(1)} %cross.1), channel_id=1, replica_groups=mesh['chan'=8,'seg'=32] {'chan','seg'}, dimensions={0} | all-to-all | bytes 3145728 | tf_op jit(solution)/shard_map/all_to_all | solution.py:206
  92.1 0.0 copy-done.1
  92.1 0.0 copy-done.2
  92.1 2.6 %lags.1 = f32[3,51,4,128]{3,2,1,0:T(4,128)} custom-call(f32[32,256]{1,0:T(8,128)S(1)} %copy-done.2, f32[32,256]{1,0:T(8,128)S(1)} %copy-done.1, s16[256,24,128]{2,1,0:T(8,128)(2,1)S(1)} %all_to_all.10.coded), custom_call_target="tpu_custom_call" | custom-call | tf_op jit(solution)/shard_map/lags/pallas_call | solution.py:206
Async XLA Ops:
  0.7 1.0 %copy-start = (bf16[4,2,200,128]{3,2,1,0:T(8,128)(2,1)S(1)}, bf16[4,2,200,128]{3,2,1,0:T(8,128)(2,1)}, u32[]{:S(2)}) copy-start(bf16[4,2,200,128]{3,2,1,0:T(8,128)(2,1)} %x.1) | copy-start | bytes 1228804
  1.7 38.2 %copy-start.3 = (s32[3,8]{1,0:T(4,128)S(1)}, s32[3,8]{1,0:T(4,128)}, u32[]{:S(2)}) copy-start(s32[3,8]{1,0:T(4,128)} %match.1) | copy-start | bytes 292
  2.7 37.1 %all-to-all-start = ((bf16[256,8,128]{2,1,0:T(8,128)(2,1)}), bf16[256,8,128]{2,1,0:T(8,128)(2,1)S(1)}, u32[]{:S(2)}, u32[]{:S(2)}) async-start(bf16[256,8,128]{2,1,0:T(8,128)(2,1)} %send.1), calls=%async_computation | async-start | bytes 1048576 | tf_op jit(solution)/shard_map/all_to_all | solution.py:203
  43.0 49.1 %copy-start.1 = (f32[32,256]{1,0:T(8,128)S(1)}, f32[32,256]{1,0:T(8,128)}, u32[]{:S(2)}) copy-start(f32[32,256]{1,0:T(8,128)} %constant.16.clone.sin) | copy-start | bytes 98308
  43.1 49.1 %copy-start.2 = (f32[32,256]{1,0:T(8,128)S(1)}, f32[32,256]{1,0:T(8,128)}, u32[]{:S(2)}) copy-start(f32[32,256]{1,0:T(8,128)} %constant.15.clone.cos) | copy-start | bytes 98308

commit v4 on v3

--- a/solution.py
+++ b/solution.py
@@ -15,7 +15,7 @@
 ROWS = 32
 LANES = 128
 
-KNEE = 2.0**-10
+KNEE = 2.0**-16
 TOP = 32000.0
 UNIT = 8192.0
 
@@ -111,7 +111,7 @@
     rows = coded.shape[1]
     tile = rows // ROUNDS
     half = tile // 2
-    x[...] = coded[...].astype(jnp.int32).reshape(x.shape)
+    x[: bins * rows] = coded[...].astype(jnp.int32).reshape(bins * rows, LANES)
 
     at = (freq + 1) * rows
     power = x[at : at + tile, :].astype(jnp.float32)
@@ -185,7 +185,7 @@
         out_shape=jax.ShapeDtypeStruct((ROUNDS, LAGS, tile // 2, block), jnp.float32),
         in_specs=[vmem] * 3,
         out_specs=vmem,
-        scratch_shapes=[pltpu.VMEM((bins * rows, block), jnp.int32)],
+        scratch_shapes=[pltpu.VMEM(((bins + 1) * rows, block), jnp.int32)],
         compiler_params=params,
         name="lags",
     )

time: 95 us -> 95 us (level)
  no operation moved by 1% of the time
where the time goes in v4:
time: 95 us; the launch traced here: 94.7 us
  blocking collectives  49 us (52%)
  waiting for transfers between devices  21.4 us (23%)
  starting transfers between devices  15.7 us (17%)
  Pallas kernels  6.9 us (7%)
  local copies, waits for them, and re-layouts  1.01 us (1%)
    all_to_all x1, blocking collectives, on_device(): return lags(lax.all_to_all(coded, ('chan', 'seg'), 0, 0, tiled=True))  49 us
    all_to_all x1, waiting for transfers between devices, on_device(): lax.all_to_all(send(counts, spectra), ('chan', 'seg'), 0, 0, tiled=True)  21.4 us
    all_to_all x1, starting transfers between devices, on_device(): lax.all_to_all(send(counts, spectra), ('chan', 'seg'), 0, 0, tiled=True)  15.7 us
    pallas_call x1, Pallas kernels, on_device(): coded = cross(place.astype(jnp.int32).reshape(1), match, here)  3.2 us
    pallas_call x1, Pallas kernels, on_device(): return lags(lax.all_to_all(coded, ('chan', 'seg'), 0, 0, tiled=True))  2.62 us
  transfers between devices with their start and end apart: 1, of which 1 were waited for; matrix products, arithmetic and copies ran while one was open for 0% of the time, Pallas kernels for 0%

profile of v4, /device:TPU:1, one launch (start us, length us, event | category | flops | bytes accessed | tf_op | source)
XLA Modules:
  0.0 94.7 jit_solution(11763503153956494901)
XLA Ops:
  0.7 0.0 copy-start
  0.7 1.0 %copy-done = bf16[4,2,200,128]{3,2,1,0:T(8,128)(2,1)S(1)} copy-done((bf16[4,2,200,128]{3,2,1,0:T(8,128)(2,1)S(1)}, bf16[4,2,200,128]{3,2,1,0:T(8,128)(2,1)}, u32[]{:S(2)}) %copy-start) | copy-done | bytes 409624
  1.7 0.0 copy-start.3
  1.7 1.1 %send.1 = bf16[256,8,128]{2,1,0:T(8,128)(2,1)} custom-call(s32[1]{0:T(128)S(6)} %copy.6.counts, bf16[4,2,200,128]{3,2,1,0:T(8,128)(2,1)S(1)} %copy-done), custom_call_target="tpu_custom_call" | custom-call | tf_op jit(solution)/shard_map/send/pallas_call | solution.py:203
  2.7 15.7 %all-to-all-start = ((bf16[256,8,128]{2,1,0:T(8,128)(2,1)}), bf16[256,8,128]{2,1,0:T(8,128)(2,1)S(1)}, u32[]{:S(2)}, u32[]{:S(2)}) async-start(bf16[256,8,128]{2,1,0:T(8,128)(2,1)} %send.1), calls=%async_computation | async-start | bytes 1048576 | tf_op jit(solution)/shard_map/all_to_all | solution.py:203
  18.4 21.4 %all-to-all-done = bf16[256,8,128]{2,1,0:T(8,128)(2,1)S(1)} async-done(((bf16[256,8,128]{2,1,0:T(8,128)(2,1)}), bf16[256,8,128]{2,1,0:T(8,128)(2,1)S(1)}, u32[]{:S(2)}, u32[]{:S(2)}) %all-to-all-start) | async-done | bytes 524320 | tf_op jit(solution)/shard_map/all_to_all | solution.py:203
  39.8 0.0 copy-done.3
  39.8 3.2 %cross.1 = s16[256,24,128]{2,1,0:T(8,128)(2,1)S(1)} custom-call(s32[1]{0:T(128)} %bitcast.place, s32[3,8]{1,0:T(4,128)S(1)} %copy-done.3, bf16[8,256,128]{2,1,0:T(8,128)(2,1)S(1)} %bitcast.2), custom_call_target="tpu_custom_call" | custom-call | tf_op jit(solution)/shard_map/cross/pallas_call | solution.py:205
  43.0 0.0 copy-start.1
  43.1 0.0 copy-start.2
  43.1 49.0 %all_to_all.10.coded = s16[256,24,128]{2,1,0:T(8,128)(2,1)S(1)} all-to-all(s16[256,24,128]{2,1,0:T(8,128)(2,1)S(1)} %cross.1), channel_id=1, replica_groups=mesh['chan'=8,'seg'=32] {'chan','seg'}, dimensions={0} | all-to-all | bytes 3145728 | tf_op jit(solution)/shard_map/all_to_all | solution.py:206
  92.1 0.0 copy-done.1
  92.1 0.0 copy-done.2
  92.1 2.6 %lags.1 = f32[3,51,4,128]{3,2,1,0:T(4,128)} custom-call(f32[32,256]{1,0:T(8,128)S(1)} %copy-done.2, f32[32,256]{1,0:T(8,128)S(1)} %copy-done.1, s16[256,24,128]{2,1,0:T(8,128)(2,1)S(1)} %all_to_all.10.coded), custom_call_target="tpu_custom_call" | custom-call | tf_op jit(solution)/shard_map/lags/pallas_call | solution.py:206
Async XLA Ops:
  0.7 1.0 %copy-start = (bf16[4,2,200,128]{3,2,1,0:T(8,128)(2,1)S(1)}, bf16[4,2,200,128]{3,2,1,0:T(8,128)(2,1)}, u32[]{:S(2)}) copy-start(bf16[4,2,200,128]{3,2,1,0:T(8,128)(2,1)} %x.1) | copy-start | bytes 1228804
  1.7 38.2 %copy-start.3 = (s32[3,8]{1,0:T(4,128)S(1)}, s32[3,8]{1,0:T(4,128)}, u32[]{:S(2)}) copy-start(s32[3,8]{1,0:T(4,128)} %match.1) | copy-start | bytes 292
  2.7 37.1 %all-to-all-start = ((bf16[256,8,128]{2,1,0:T(8,128)(2,1)}), bf16[256,8,128]{2,1,0:T(8,128)(2,1)S(1)}, u32[]{:S(2)}, u32[]{:S(2)}) async-start(bf16[256,8,128]{2,1,0:T(8,128)(2,1)} %send.1), calls=%async_computation | async-start | bytes 1048576 | tf_op jit(solution)/shard_map/all_to_all | solution.py:203
  43.0 49.1 %copy-start.1 = (f32[32,256]{1,0:T(8,128)S(1)}, f32[32,256]{1,0:T(8,128)}, u32[]{:S(2)}) copy-start(f32[32,256]{1,0:T(8,128)} %constant.16.clone.sin) | copy-start | bytes 98308
  43.1 49.1 %copy-start.2 = (f32[32,256]{1,0:T(8,128)S(1)}, f32[32,256]{1,0:T(8,128)}, u32[]{:S(2)}) copy-start(f32[32,256]{1,0:T(8,128)} %constant.15.clone.cos) | copy-start | bytes 98308

commit v5 on v4

--- a/solution.py
+++ b/solution.py
@@ -29,6 +29,12 @@
         np.where(live, np.cos(angle), 0.0).astype(np.float32),
         np.where(live, np.sin(angle), 0.0).astype(np.float32),
     )
+
+
+def ranks(chans, segs):
+    outer = segs // 2
+    inner = chans * segs // outer
+    return [i + outer * j for i in range(outer) for j in range(inner)]
 
 
 def per_e(depth):
@@ -56,18 +62,23 @@
     out[...] = rows[...].astype(jnp.bfloat16).reshape(out.shape)
 
 
-def cross_kernel(freq, place, match, x, out):
+def cross_kernel(freq, order, place, match, received, out, x):
     blocks, depth, block = x.shape
     bins, rows, _ = out.shape
     sources = bins // blocks
     tile = rows // ROUNDS
     half = tile // 2
+    at = {device: i for i, device in enumerate(order)}
+
+    for c in range(blocks):
+        own = [received[at[c * sources + i]].astype(jnp.float32) for i in range(sources)]
+        x[c] = jnp.concatenate(own, axis=0).astype(jnp.bfloat16)
 
     row = lax.broadcasted_iota(jnp.int32, (2 * block, 2 * block), 0)
     col = lax.broadcasted_iota(jnp.int32, (2 * block, 2 * block), 1)
     channel = (row // tile) * half + row % half
     part = (row % tile) // half
-    order = (col == part * block + channel).astype(jnp.bfloat16)
+    select = (col == part * block + channel).astype(jnp.bfloat16)
     most = jnp.max(jnp.abs(x[...].astype(jnp.float32)))
     inverse = jnp.where(most > 0.0, 1.0 / jnp.maximum(most, 1e-37), 0.0)
 
@@ -77,7 +88,7 @@
         swapped = jnp.concatenate([groups[:, half:], -groups[:, :half]], axis=1)
         both = jnp.concatenate([own, swapped.reshape(depth, block).astype(jnp.bfloat16)], axis=1)
         turned = lax.dot_general(
-            order, both, (((1,), (1,)), ((), ())), preferred_element_type=jnp.float32
+            select, both, (((1,), (1,)), ((), ())), preferred_element_type=jnp.float32
         ).astype(jnp.bfloat16)
         coded = []
         for r in range(ROUNDS):
@@ -86,12 +97,13 @@
             code = (jnp.log(1.0 + jnp.abs(y)) * per_e(depth) + 0.5).astype(jnp.int32)
             code = jnp.where(y < 0.0, -code, code)
             coded.append(code.astype(jnp.int16).reshape(sources, tile, block))
-        out[pl.ds(c * sources, sources)] = jnp.concatenate(coded, axis=1)
+        for i in range(sources):
+            out[at[c * sources + i]] = jnp.concatenate([code[i] for code in coded], axis=0)
 
     for c in range(blocks):
         one(c)
 
-    @pl.when(place[0] == freq + 1)
+    @pl.when(place[0] == order[freq + 1])
     def _():
         most = jnp.max(x[...].astype(jnp.float32).reshape(blocks * sources, tile, block), axis=0)
         power = jnp.floor(jnp.log2(jnp.maximum(most, 1e-37)))
@@ -173,10 +185,11 @@
         name="send",
     )
     cross = pl.pallas_call(
-        functools.partial(cross_kernel, freq),
+        functools.partial(cross_kernel, freq, ranks(chans, segs)),
         out_shape=jax.ShapeDtypeStruct((bins, rows, block), jnp.int16),
         in_specs=[smem, smem, vmem],
         out_specs=vmem,
+        scratch_shapes=[pltpu.VMEM((chans, depth, block), jnp.bfloat16)],
         compiler_params=params,
         name="cross",
     )
@@ -198,12 +211,12 @@
     chans = lax.axis_size("chan")
     segs = lax.axis_size("seg")
     place = lax.axis_index("chan") * segs + lax.axis_index("seg")
+    groups = [ranks(chans, segs)]
     send, cross, lags = kernels(slots, parts, freq, block, chans, segs)
 
-    here = lax.all_to_all(send(counts, spectra), ("chan", "seg"), 0, 0, tiled=True)
-    here = here.reshape(chans, segs * slots * parts, block)
+    here = lax.all_to_all(send(counts, spectra), ("chan", "seg"), 0, 0, axis_index_groups=groups, tiled=True)
     coded = cross(place.astype(jnp.int32).reshape(1), match, here)
-    return lags(lax.all_to_all(coded, ("chan", "seg"), 0, 0, tiled=True))
+    return lags(lax.all_to_all(coded, ("chan", "seg"), 0, 0, axis_index_groups=groups, tiled=True))
 
 
 def solution(mesh):

time: 95 us -> 91.7 us (0.965)
  blocking collectives: 49 us -> 46.2 us
    all_to_all x1, blocking collectives: 49 us -> 46.2 us  [on_device(): lax.all_to_all(coded, ('chan', 'seg'), 0, 0, axis_index_groups=groups, ti...]
where the time goes in v5:
time: 91.7 us; the launch traced here: 91.3 us
  blocking collectives  46.2 us (50%)
  waiting for transfers between devices  20.8 us (23%)
  starting transfers between devices  15.7 us (17%)
  Pallas kernels  6.96 us (8%)
  local copies, waits for them, and re-layouts  1.01 us (1%)
    all_to_all x1, blocking collectives, on_device(): lax.all_to_all(coded, ('chan', 'seg'), 0, 0, axis_index_groups=groups, ti...  46.2 us
    all_to_all x1, waiting for transfers between devices, on_device(): lax.all_to_all(send(counts, spectra), ('chan', 'seg'), 0, 0, axis_index_g...  20.8 us
    all_to_all x1, starting transfers between devices, on_device(): lax.all_to_all(send(counts, spectra), ('chan', 'seg'), 0, 0, axis_index_g...  15.7 us
    pallas_call x1, Pallas kernels, on_device(): coded = cross(place.astype(jnp.int32).reshape(1), match, here)  3.26 us
    pallas_call x1, Pallas kernels, on_device(): lags(lax.all_to_all(coded, ('chan', 'seg'), 0, 0, axis_index_groups=group...  2.62 us
  transfers between devices with their start and end apart: 1, of which 1 were waited for; matrix products, arithmetic and copies ran while one was open for 0% of the time, Pallas kernels for 0%

profile of v5, /device:TPU:1, one launch (start us, length us, event | category | flops | bytes accessed | tf_op | source)
XLA Modules:
  0.0 91.3 jit_solution(2444698869247519995)
XLA Ops:
  0.7 0.0 copy-start
  0.7 1.0 %copy-done = bf16[4,2,200,128]{3,2,1,0:T(8,128)(2,1)S(1)} copy-done((bf16[4,2,200,128]{3,2,1,0:T(8,128)(2,1)S(1)}, bf16[4,2,200,128]{3,2,1,0:T(8,128)(2,1)}, u32[]{:S(2)}) %copy-start) | copy-done | bytes 409624
  1.7 0.0 copy-start.3
  1.7 1.1 %send.1 = bf16[256,8,128]{2,1,0:T(8,128)(2,1)} custom-call(s32[1]{0:T(128)S(6)} %copy.6.counts, bf16[4,2,200,128]{3,2,1,0:T(8,128)(2,1)S(1)} %copy-done), custom_call_target="tpu_custom_call" | custom-call | tf_op jit(solution)/shard_map/send/pallas_call | solution.py:217
  2.7 15.7 %all-to-all-start = ((bf16[256,8,128]{2,1,0:T(8,128)(2,1)}), bf16[256,8,128]{2,1,0:T(8,128)(2,1)S(1)}, u32[]{:S(2)}, u32[]{:S(2)}) async-start(bf16[256,8,128]{2,1,0:T(8,128)(2,1)} %send.1), calls=%async_computation | async-start | bytes 1048576 | tf_op jit(solution)/shard_map/all_to_all | solution.py:217
  18.4 20.8 %all-to-all-done.received = bf16[256,8,128]{2,1,0:T(8,128)(2,1)S(1)} async-done(((bf16[256,8,128]{2,1,0:T(8,128)(2,1)}), bf16[256,8,128]{2,1,0:T(8,128)(2,1)S(1)}, u32[]{:S(2)}, u32[]{:S(2)}) %all-to-all-start) | async-done | bytes 524320 | tf_op jit(solution)/shard_map/all_to_all | solution.py:217
  39.2 0.0 copy-done.3
  39.2 3.3 %cross.1 = s16[256,24,128]{2,1,0:T(8,128)(2,1)S(1)} custom-call(s32[1]{0:T(128)} %bitcast.place, s32[3,8]{1,0:T(4,128)S(1)} %copy-done.3, bf16[256,8,128]{2,1,0:T(8,128)(2,1)S(1)} %all-to-all-done.received), custom_call_target="tpu_custom_call" | custom-call | tf_op jit(solution)/shard_map/cross/pallas_call | solution.py:218
  42.5 0.0 copy-start.1
  42.5 0.0 copy-start.2
  42.5 46.2 %all_to_all.10.coded = s16[256,24,128]{2,1,0:T(8,128)(2,1)S(1)} all-to-all(s16[256,24,128]{2,1,0:T(8,128)(2,1)S(1)} %cross.1), channel_id=1, replica_groups={{0,16,32,48,64,80,96,112,128,144,160,176,192,208,224,240,1,17,33,49,65,..., dimensions={0} | all-to-all | bytes 3145728 | tf_op jit(solution)/shard_map/all_to_all | solution.py:219
  88.7 0.0 copy-done.1
  88.7 0.0 copy-done.2
  88.7 2.6 %lags.1 = f32[3,51,4,128]{3,2,1,0:T(4,128)} custom-call(f32[32,256]{1,0:T(8,128)S(1)} %copy-done.2, f32[32,256]{1,0:T(8,128)S(1)} %copy-done.1, s16[256,24,128]{2,1,0:T(8,128)(2,1)S(1)} %all_to_all.10.coded), custom_call_target="tpu_custom_call" | custom-call | tf_op jit(solution)/shard_map/lags/pallas_call | solution.py:219
Async XLA Ops:
  0.7 1.0 %copy-start = (bf16[4,2,200,128]{3,2,1,0:T(8,128)(2,1)S(1)}, bf16[4,2,200,128]{3,2,1,0:T(8,128)(2,1)}, u32[]{:S(2)}) copy-start(bf16[4,2,200,128]{3,2,1,0:T(8,128)(2,1)} %x.1) | copy-start | bytes 1228804
  1.7 37.6 %copy-start.3 = (s32[3,8]{1,0:T(4,128)S(1)}, s32[3,8]{1,0:T(4,128)}, u32[]{:S(2)}) copy-start(s32[3,8]{1,0:T(4,128)} %match.1) | copy-start | bytes 292
  2.7 36.5 %all-to-all-start = ((bf16[256,8,128]{2,1,0:T(8,128)(2,1)}), bf16[256,8,128]{2,1,0:T(8,128)(2,1)S(1)}, u32[]{:S(2)}, u32[]{:S(2)}) async-start(bf16[256,8,128]{2,1,0:T(8,128)(2,1)} %send.1), calls=%async_computation | async-start | bytes 1048576 | tf_op jit(solution)/shard_map/all_to_all | solution.py:217
  42.5 46.2 %copy-start.1 = (f32[32,256]{1,0:T(8,128)S(1)}, f32[32,256]{1,0:T(8,128)}, u32[]{:S(2)}) copy-start(f32[32,256]{1,0:T(8,128)} %constant.16.clone.sin) | copy-start | bytes 98308
  42.5 46.2 %copy-start.2 = (f32[32,256]{1,0:T(8,128)S(1)}, f32[32,256]{1,0:T(8,128)}, u32[]{:S(2)}) copy-start(f32[32,256]{1,0:T(8,128)} %constant.15.clone.cos) | copy-start | bytes 98308

commit v6 on v5

--- a/solution.py
+++ b/solution.py
@@ -32,9 +32,13 @@
 
 
 def ranks(chans, segs):
-    outer = segs // 2
-    inner = chans * segs // outer
-    return [i + outer * j for i in range(outer) for j in range(inner)]
+    low = segs // 2
+
+    def key(device):
+        chan, seg = device // segs, device % segs
+        return chan // 2 % 2, chan % 2, chan // 4, seg % low, seg // low
+
+    return sorted(range(chans * segs), key=key)
 
 
 def per_e(depth):
@@ -123,13 +127,13 @@
     rows = coded.shape[1]
     tile = rows // ROUNDS
     half = tile // 2
-    x[: bins * rows] = coded[...].astype(jnp.int32).reshape(bins * rows, LANES)
+    x[: bins * rows] = coded[:bins].astype(jnp.int32).reshape(bins * rows, LANES)
 
     at = (freq + 1) * rows
     power = x[at : at + tile, :].astype(jnp.float32)
     share = x[at + tile : at + 2 * tile, :].astype(jnp.float32)
     most = share * jnp.exp2(power) * (1.0 / UNIT)
-    most = jnp.concatenate([most[i : i + 1] for i in range(bins // LANES)], axis=1)
+    most = jnp.concatenate([most[:1], most[1:2]], axis=1)[:, :bins]
 
     def both(table):
         high, low = split(table[...] * most * most * KNEE)
@@ -170,6 +174,7 @@
     tile = slots * parts
     depth = segs * tile
     rows = ROUNDS * tile
+    used = min(bins, (freq + 2 + 15) // 16 * 16)
 
     vmem = pl.BlockSpec(memory_space=pltpu.VMEM)
     smem = pl.BlockSpec(memory_space=pltpu.SMEM)
@@ -198,11 +203,11 @@
         out_shape=jax.ShapeDtypeStruct((ROUNDS, LAGS, tile // 2, block), jnp.float32),
         in_specs=[vmem] * 3,
         out_specs=vmem,
-        scratch_shapes=[pltpu.VMEM(((bins + 1) * rows, block), jnp.int32)],
+        scratch_shapes=[pltpu.VMEM(((used + 1) * rows, block), jnp.int32)],
         compiler_params=params,
         name="lags",
     )
-    cos, sin = tables(freq, bins)
+    cos, sin = tables(freq, used)
     return send, cross, functools.partial(lags, jnp.asarray(cos), jnp.asarray(sin))
 
 

time: 91.7 us -> 91 us (level)
  waiting for transfers between devices: 20.8 us -> 19.3 us
  blocking collectives: 46.2 us -> 47.5 us
    all_to_all x1, waiting for transfers between devices: 20.8 us -> 19.3 us  [on_device(): lax.all_to_all(send(counts, spectra), ('chan', 'seg'), 0, 0, axis_index_g...]
    all_to_all x1, blocking collectives: 46.2 us -> 47.5 us  [on_device(): lax.all_to_all(coded, ('chan', 'seg'), 0, 0, axis_index_groups=groups, ti...]
where the time goes in v6:
time: 91 us; the launch traced here: 90.8 us
  blocking collectives  47.5 us (52%)
  waiting for transfers between devices  19.3 us (21%)
  starting transfers between devices  15.7 us (17%)
  Pallas kernels  6.61 us (7%)
  local copies, waits for them, and re-layouts  1.01 us (1%)
    all_to_all x1, blocking collectives, on_device(): lax.all_to_all(coded, ('chan', 'seg'), 0, 0, axis_index_groups=groups, ti...  47.5 us
    all_to_all x1, waiting for transfers between devices, on_device(): lax.all_to_all(send(counts, spectra), ('chan', 'seg'), 0, 0, axis_index_g...  19.3 us
    all_to_all x1, starting transfers between devices, on_device(): lax.all_to_all(send(counts, spectra), ('chan', 'seg'), 0, 0, axis_index_g...  15.7 us
    pallas_call x1, Pallas kernels, on_device(): coded = cross(place.astype(jnp.int32).reshape(1), match, here)  3.24 us
    pallas_call x1, Pallas kernels, on_device(): lags(lax.all_to_all(coded, ('chan', 'seg'), 0, 0, axis_index_groups=group...  2.29 us
  transfers between devices with their start and end apart: 1, of which 1 were waited for; matrix products, arithmetic and copies ran while one was open for 0% of the time, Pallas kernels for 0%

profile of v6, /device:TPU:1, one launch (start us, length us, event | category | flops | bytes accessed | tf_op | source)
XLA Modules:
  0.0 90.8 jit_solution(1106465209592173320)
XLA Ops:
  0.7 0.0 copy-start
  0.7 1.0 %copy-done = bf16[4,2,200,128]{3,2,1,0:T(8,128)(2,1)S(1)} copy-done((bf16[4,2,200,128]{3,2,1,0:T(8,128)(2,1)S(1)}, bf16[4,2,200,128]{3,2,1,0:T(8,128)(2,1)}, u32[]{:S(2)}) %copy-start) | copy-done | bytes 409624
  1.7 0.0 copy-start.3
  1.7 1.1 %send.1 = bf16[256,8,128]{2,1,0:T(8,128)(2,1)} custom-call(s32[1]{0:T(128)S(6)} %copy.6.counts, bf16[4,2,200,128]{3,2,1,0:T(8,128)(2,1)S(1)} %copy-done), custom_call_target="tpu_custom_call" | custom-call | tf_op jit(solution)/shard_map/send/pallas_call | solution.py:222
  2.7 15.7 %all-to-all-start = ((bf16[256,8,128]{2,1,0:T(8,128)(2,1)}), bf16[256,8,128]{2,1,0:T(8,128)(2,1)S(1)}, u32[]{:S(2)}, u32[]{:S(2)}) async-start(bf16[256,8,128]{2,1,0:T(8,128)(2,1)} %send.1), calls=%async_computation | async-start | bytes 1048576 | tf_op jit(solution)/shard_map/all_to_all | solution.py:222
  18.4 19.3 %all-to-all-done.received = bf16[256,8,128]{2,1,0:T(8,128)(2,1)S(1)} async-done(((bf16[256,8,128]{2,1,0:T(8,128)(2,1)}), bf16[256,8,128]{2,1,0:T(8,128)(2,1)S(1)}, u32[]{:S(2)}, u32[]{:S(2)}) %all-to-all-start) | async-done | bytes 524320 | tf_op jit(solution)/shard_map/all_to_all | solution.py:222
  37.7 0.0 copy-done.3
  37.7 3.2 %cross.1 = s16[256,24,128]{2,1,0:T(8,128)(2,1)S(1)} custom-call(s32[1]{0:T(128)} %bitcast.place, s32[3,8]{1,0:T(4,128)S(1)} %copy-done.3, bf16[256,8,128]{2,1,0:T(8,128)(2,1)S(1)} %all-to-all-done.received), custom_call_target="tpu_custom_call" | custom-call | tf_op jit(solution)/shard_map/cross/pallas_call | solution.py:223
  40.9 0.0 copy-start.1
  40.9 0.0 copy-start.2
  40.9 47.5 %all_to_all.10.coded = s16[256,24,128]{2,1,0:T(8,128)(2,1)S(1)} all-to-all(s16[256,24,128]{2,1,0:T(8,128)(2,1)S(1)} %cross.1), channel_id=1, replica_groups={{0,16,1,17,2,18,3,19,4,20,5,21,6,22,7,23,8,24,9,25,10,26,11,27,12,28,13..., dimensions={0} | all-to-all | bytes 3145728 | tf_op jit(solution)/shard_map/all_to_all | solution.py:224
  88.5 0.0 copy-done.1
  88.5 0.0 copy-done.2
  88.5 2.3 %lags.1 = f32[3,51,4,128]{3,2,1,0:T(4,128)} custom-call(f32[32,208]{1,0:T(8,128)S(1)} %copy-done.2, f32[32,208]{1,0:T(8,128)S(1)} %copy-done.1, s16[256,24,128]{2,1,0:T(8,128)(2,1)S(1)} %all_to_all.10.coded), custom_call_target="tpu_custom_call" | custom-call | tf_op jit(solution)/shard_map/lags/pallas_call | solution.py:224
Async XLA Ops:
  0.7 1.0 %copy-start = (bf16[4,2,200,128]{3,2,1,0:T(8,128)(2,1)S(1)}, bf16[4,2,200,128]{3,2,1,0:T(8,128)(2,1)}, u32[]{:S(2)}) copy-start(bf16[4,2,200,128]{3,2,1,0:T(8,128)(2,1)} %x.1) | copy-start | bytes 1228804
  1.7 36.0 %copy-start.3 = (s32[3,8]{1,0:T(4,128)S(1)}, s32[3,8]{1,0:T(4,128)}, u32[]{:S(2)}) copy-start(s32[3,8]{1,0:T(4,128)} %match.1) | copy-start | bytes 292
  2.7 34.9 %all-to-all-start = ((bf16[256,8,128]{2,1,0:T(8,128)(2,1)}), bf16[256,8,128]{2,1,0:T(8,128)(2,1)S(1)}, u32[]{:S(2)}, u32[]{:S(2)}) async-start(bf16[256,8,128]{2,1,0:T(8,128)(2,1)} %send.1), calls=%async_computation | async-start | bytes 1048576 | tf_op jit(solution)/shard_map/all_to_all | solution.py:222
  40.9 47.6 %copy-start.1 = (f32[32,208]{1,0:T(8,128)S(1)}, f32[32,208]{1,0:T(8,128)}, u32[]{:S(2)}) copy-start(f32[32,208]{1,0:T(8,128)} %constant.16.clone.sin) | copy-start | bytes 79876
  40.9 47.6 %copy-start.2 = (f32[32,208]{1,0:T(8,128)S(1)}, f32[32,208]{1,0:T(8,128)}, u32[]{:S(2)}) copy-start(f32[32,208]{1,0:T(8,128)} %constant.15.clone.cos) | copy-start | bytes 79876

commit v7 on v6

--- a/solution.py
+++ b/solution.py
@@ -127,9 +127,13 @@
     rows = coded.shape[1]
     tile = rows // ROUNDS
     half = tile // 2
-    x[: bins * rows] = coded[:bins].astype(jnp.int32).reshape(bins * rows, LANES)
-
-    at = (freq + 1) * rows
+    pitch = rows + 1
+    groups = coded[:bins].reshape(bins // 8, 8, rows, LANES)
+    for i in range(8):
+        x[: bins // 8, i * pitch : i * pitch + rows, :] = groups[:, i].astype(jnp.int32)
+    x = x.reshape((bins // 8 + 1) * 8 * pitch, LANES)
+
+    at = (freq + 1) * pitch
     power = x[at : at + tile, :].astype(jnp.float32)
     share = x[at + tile : at + 2 * tile, :].astype(jnp.float32)
     most = share * jnp.exp2(power) * (1.0 / UNIT)
@@ -145,7 +149,7 @@
         return first[:ROWS] + first[ROWS:] + jnp.dot(tables[1], low, preferred_element_type=jnp.float32)
 
     def load(at):
-        code = x[pl.ds(at, bins, stride=rows), :].astype(jnp.float32)
+        code = x[pl.ds(at, bins, stride=pitch), :].astype(jnp.float32)
         size = jnp.exp(jnp.abs(code) * (1.0 / per_e(depth))) - 1.0
         return jnp.where(code < 0.0, -size, size)
 
@@ -203,7 +207,7 @@
         out_shape=jax.ShapeDtypeStruct((ROUNDS, LAGS, tile // 2, block), jnp.float32),
         in_specs=[vmem] * 3,
         out_specs=vmem,
-        scratch_shapes=[pltpu.VMEM(((used + 1) * rows, block), jnp.int32)],
+        scratch_shapes=[pltpu.VMEM((used // 8 + 1, 8 * (rows + 1), block), jnp.int32)],
         compiler_params=params,
         name="lags",
     )

time: 91 us -> 90.9 us (level)
  no operation moved by 1% of the time
where the time goes in v7:
time: 90.9 us; the launch traced here: 90.6 us
  blocking collectives  47.5 us (52%)
  waiting for transfers between devices  19.3 us (21%)
  starting transfers between devices  15.7 us (17%)
  Pallas kernels  6.47 us (7%)
  local copies, waits for them, and re-layouts  1.01 us (1%)
    all_to_all x1, blocking collectives, on_device(): lax.all_to_all(coded, ('chan', 'seg'), 0, 0, axis_index_groups=groups, ti...  47.5 us
    all_to_all x1, waiting for transfers between devices, on_device(): lax.all_to_all(send(counts, spectra), ('chan', 'seg'), 0, 0, axis_index_g...  19.3 us
    all_to_all x1, starting transfers between devices, on_device(): lax.all_to_all(send(counts, spectra), ('chan', 'seg'), 0, 0, axis_index_g...  15.7 us
    pallas_call x1, Pallas kernels, on_device(): coded = cross(place.astype(jnp.int32).reshape(1), match, here)  3.24 us
    pallas_call x1, Pallas kernels, on_device(): lags(lax.all_to_all(coded, ('chan', 'seg'), 0, 0, axis_index_groups=group...  2.15 us
  transfers between devices with their start and end apart: 1, of which 1 were waited for; matrix products, arithmetic and copies ran while one was open for 0% of the time, Pallas kernels for 0%

profile of v7, /device:TPU:1, one launch (start us, length us, event | category | flops | bytes accessed | tf_op | source)
XLA Modules:
  0.0 90.6 jit_solution(7165370372441639695)
XLA Ops:
  0.7 0.0 copy-start
  0.7 1.0 %copy-done = bf16[4,2,200,128]{3,2,1,0:T(8,128)(2,1)S(1)} copy-done((bf16[4,2,200,128]{3,2,1,0:T(8,128)(2,1)S(1)}, bf16[4,2,200,128]{3,2,1,0:T(8,128)(2,1)}, u32[]{:S(2)}) %copy-start) | copy-done | bytes 409624
  1.7 0.0 copy-start.3
  1.7 1.1 %send.1 = bf16[256,8,128]{2,1,0:T(8,128)(2,1)} custom-call(s32[1]{0:T(128)S(6)} %copy.6.counts, bf16[4,2,200,128]{3,2,1,0:T(8,128)(2,1)S(1)} %copy-done), custom_call_target="tpu_custom_call" | custom-call | tf_op jit(solution)/shard_map/send/pallas_call | solution.py:226
  2.7 15.7 %all-to-all-start = ((bf16[256,8,128]{2,1,0:T(8,128)(2,1)}), bf16[256,8,128]{2,1,0:T(8,128)(2,1)S(1)}, u32[]{:S(2)}, u32[]{:S(2)}) async-start(bf16[256,8,128]{2,1,0:T(8,128)(2,1)} %send.1), calls=%async_computation | async-start | bytes 1048576 | tf_op jit(solution)/shard_map/all_to_all | solution.py:226
  18.4 19.3 %all-to-all-done.received = bf16[256,8,128]{2,1,0:T(8,128)(2,1)S(1)} async-done(((bf16[256,8,128]{2,1,0:T(8,128)(2,1)}), bf16[256,8,128]{2,1,0:T(8,128)(2,1)S(1)}, u32[]{:S(2)}, u32[]{:S(2)}) %all-to-all-start) | async-done | bytes 524320 | tf_op jit(solution)/shard_map/all_to_all | solution.py:226
  37.7 0.0 copy-done.3
  37.7 3.2 %cross.1 = s16[256,24,128]{2,1,0:T(8,128)(2,1)S(1)} custom-call(s32[1]{0:T(128)} %bitcast.place, s32[3,8]{1,0:T(4,128)S(1)} %copy-done.3, bf16[256,8,128]{2,1,0:T(8,128)(2,1)S(1)} %all-to-all-done.received), custom_call_target="tpu_custom_call" | custom-call | tf_op jit(solution)/shard_map/cross/pallas_call | solution.py:227
  40.9 0.0 copy-start.1
  40.9 0.0 copy-start.2
  40.9 47.5 %all_to_all.10.coded = s16[256,24,128]{2,1,0:T(8,128)(2,1)S(1)} all-to-all(s16[256,24,128]{2,1,0:T(8,128)(2,1)S(1)} %cross.1), channel_id=1, replica_groups={{0,16,1,17,2,18,3,19,4,20,5,21,6,22,7,23,8,24,9,25,10,26,11,27,12,28,13..., dimensions={0} | all-to-all | bytes 3145728 | tf_op jit(solution)/shard_map/all_to_all | solution.py:228
  88.5 0.0 copy-done.1
  88.5 0.0 copy-done.2
  88.5 2.2 %lags.1 = f32[3,51,4,128]{3,2,1,0:T(4,128)} custom-call(f32[32,208]{1,0:T(8,128)S(1)} %copy-done.2, f32[32,208]{1,0:T(8,128)S(1)} %copy-done.1, s16[256,24,128]{2,1,0:T(8,128)(2,1)S(1)} %all_to_all.10.coded), custom_call_target="tpu_custom_call" | custom-call | tf_op jit(solution)/shard_map/lags/pallas_call | solution.py:228
Async XLA Ops:
  0.7 1.0 %copy-start = (bf16[4,2,200,128]{3,2,1,0:T(8,128)(2,1)S(1)}, bf16[4,2,200,128]{3,2,1,0:T(8,128)(2,1)}, u32[]{:S(2)}) copy-start(bf16[4,2,200,128]{3,2,1,0:T(8,128)(2,1)} %x.1) | copy-start | bytes 1228804
  1.7 36.0 %copy-start.3 = (s32[3,8]{1,0:T(4,128)S(1)}, s32[3,8]{1,0:T(4,128)}, u32[]{:S(2)}) copy-start(s32[3,8]{1,0:T(4,128)} %match.1) | copy-start | bytes 292
  2.7 34.9 %all-to-all-start = ((bf16[256,8,128]{2,1,0:T(8,128)(2,1)}), bf16[256,8,128]{2,1,0:T(8,128)(2,1)S(1)}, u32[]{:S(2)}, u32[]{:S(2)}) async-start(bf16[256,8,128]{2,1,0:T(8,128)(2,1)} %send.1), calls=%async_computation | async-start | bytes 1048576 | tf_op jit(solution)/shard_map/all_to_all | solution.py:226
  40.9 47.6 %copy-start.1 = (f32[32,208]{1,0:T(8,128)S(1)}, f32[32,208]{1,0:T(8,128)}, u32[]{:S(2)}) copy-start(f32[32,208]{1,0:T(8,128)} %constant.16.clone.sin) | copy-start | bytes 79876
  40.9 47.6 %copy-start.2 = (f32[32,208]{1,0:T(8,128)S(1)}, f32[32,208]{1,0:T(8,128)}, u32[]{:S(2)}) copy-start(f32[32,208]{1,0:T(8,128)} %constant.15.clone.cos) | copy-start | bytes 79876
